TPU v7x, 32 devices: a whole 2x2x4 slice. The times are simulated.
32 devices in a mesh: parts: 2 (over y), seq: 4 (over z), head: 2 (over x), sub: 2 (over core).
Axes of the slice: x: 2, y: 2, z: 4, core: 2. Of those that a mesh axis runs over, the one named last changes fastest.
Arguments:
- queries: bfloat16 [4096, 24576], P(('parts', 'seq'), ('head', 'sub')), parts along dimension 0, may hold values from -16 to 16
- keys: bfloat16 [4096, 24576], P(('parts', 'seq'), ('head', 'sub')), parts along dimension 0, may hold values from -6 to 6
- values: bfloat16 [4096, 16384], P(('parts', 'seq'), ('head', 'sub')), parts along dimension 0, may hold values from -6 to 6
- gates: float32 [3, 4096, 128], P(None, ('parts', 'seq'), ('head', 'sub')), parts along dimension 1, may hold values from 0.1 to 1
- pool_keys: float32 [128, 32], P(('head', 'sub')), may hold values from -1 to 1
- pool_values: float32 [128, 32], P(('head', 'sub')), may hold values from -1 to 1
- windows: int32 [128], P(('head', 'sub')), may hold values from 64 to 256, as said below
- selected: int32 [32, 8], P('parts'), parts along dimension 0, may hold values from -1 to 31, as said below
Outputs:
- attended: bfloat16 [4096, 16384], P(('parts', 'seq'), ('head', 'sub')), parts along dimension 0
There are 2 independent parts, one for each index of `parts`. A program takes and returns all parts, laid end to end along the dimension named above; an argument that names none is the same for every part. Nothing has to cross between parts.
Inputs may be any that keep to these rules, and one draw needn't show every extreme that they name: `selected`: row b begins with its own 128 // 64 blocks b * 2 onward; the further entries are distinct blocks of positions before the device of 512 positions that holds query block b, or -1 (unused). All query blocks held by one device name at most one block of any other device of 512 positions, the same one. `windows`: one head has the longest window.
All inputs are finite; a program needn't handle non-finite values.
Results may differ from a plain program's by a relative error of at most 0.0095.
Values may be sent and summed in bfloat16 or wider, within the bound.
No kernel may reach another device: no remote copies, remote signals or barrier semaphores. Data moves between devices by JAX's collectives and lax.ppermute only.
A program may use at most 192 MiB of HBM per device.

v0:
```python
import functools
import math

import jax
import jax.numpy as jnp
from jax import lax
from jax.experimental import pallas as pl
from jax.experimental.pallas import tpu as pltpu
from jax.sharding import PartitionSpec as P

DK = 192
DV = 128
CB = 32
SB = 64
QB = 128
NSEL = 8
WIN_MAX = 256
LANES = 128
PK = 2 * DK
PV = 2 * DV
NEG = -1e30
RATE = DK ** (-0.5) * math.log2(math.e)
BF = jnp.bfloat16
F32 = jnp.float32
UNIT = 16
POOL_PAIRS = 2
MERGE_ROWS = 64
VMEM = 60 * 1024 * 1024
CHEAP = pl.CostEstimate(flops=1, bytes_accessed=1, transcendentals=0)


def passed_along(value, axis, steps, first=0):
    count = lax.axis_size(axis)
    leading, last = (max(first, -steps), min(count, count - steps))
    return lax.ppermute(value, axis, [(source, source + steps) for source in range(leading, last)])


def dot_t(a, b):
    return lax.dot_general(a, b, (((1,), (1,)), ((), ())), preferred_element_type=F32)


def dot(a, b):
    return lax.dot_general(a, b, (((1,), (0,)), ((), ())), preferred_element_type=F32)


def lane_of(shape):
    return lax.broadcasted_iota(jnp.int32, shape, len(shape) - 1)


def head_lanes(block, which):
    wide = 2 * LANES
    part = block[:, which * LANES : which * LANES + wide]
    lane = lane_of(part.shape)
    keep = (lane < DK) if which == 0 else (lane >= wide - DK)
    return jnp.where(keep, part, jnp.zeros_like(part))


def column(table, head):
    return jnp.sum(jnp.where(lane_of(table.shape) == head, table, 0.0), axis=-1, keepdims=True)


def gap_biases(window):
    gap = lax.broadcasted_iota(jnp.int32, (QB, QB), 0) - lax.broadcasted_iota(jnp.int32, (QB, QB), 1)
    causal = gap >= 0
    b0 = jnp.where(causal & (gap < window), 0.0, NEG)
    b1 = jnp.where(gap < window - QB, 0.0, NEG)
    b2 = jnp.where(gap < window - 2 * QB, 0.0, NEG)
    return b0, b1, b2, jnp.where(causal, 0.0, NEG)


def pack_body(steps, with_q, owners, sel_ref, q_ref, k_ref, v_ref, *rest):
    far = len(steps)
    outs, (held, held_q, sem_in, sem_out) = rest[: far + with_q], rest[far + with_q :]
    feat_k = k_ref.shape[1]
    per_owner = k_ref.shape[0] // SB
    q_here = sel_ref.shape[1] // owners
    rank = lax.axis_index("seq")
    moves = []
    for d, step in enumerate(steps):
        user = jnp.minimum(rank + step, owners - 1)
        block = jnp.int32(0)
        for b in range(q_here):
            for e in range(NSEL):
                entry = sel_ref[e, user * q_here + b] - rank * per_owner
                block = jnp.where((entry >= 0) & (entry < per_owner), entry, block)
        rows = pl.ds(pl.multiple_of(block * SB, SB), SB)
        for ref, lanes in ((k_ref, pl.ds(0, feat_k)), (v_ref, pl.ds(feat_k, v_ref.shape[1]))):
            moves.append((ref.at[rows], held.at[d, :, lanes], outs[d].at[:, lanes]))
    if with_q:
        for r in range(0, WIN_MAX, SB):
            rows = pl.ds(r, SB)
            moves.append((q_ref.at[rows], held_q.at[rows], outs[far].at[rows]))
    inward = [pltpu.make_async_copy(m[0], m[1], sem_in.at[n]) for n, m in enumerate(moves)]
    outward = [pltpu.make_async_copy(m[1], m[2], sem_out.at[n]) for n, m in enumerate(moves)]
    for copy in inward:
        copy.start()
    for one, other in zip(inward, outward):
        one.wait()
        other.start()
    for copy in outward:
        copy.wait()


def pack(steps, with_q, owners, selected, queries, keys, values):
    far = len(steps)
    anywhere = pl.BlockSpec(memory_space=pl.ANY)
    width = keys.shape[1] + values.shape[1]
    count = 2 * far + WIN_MAX // SB
    shapes = [jax.ShapeDtypeStruct((SB, width), BF)] * far
    shapes += [jax.ShapeDtypeStruct((WIN_MAX, queries.shape[1]), BF)] * with_q
    return pl.pallas_call(
        functools.partial(pack_body, steps, with_q, owners),
        in_specs=[pl.BlockSpec(memory_space=pltpu.SMEM)] + [anywhere] * 3,
        out_specs=[anywhere] * len(shapes),
        out_shape=shapes,
        scratch_shapes=[
            pltpu.VMEM((far, SB, width), BF),
            pltpu.VMEM((WIN_MAX if with_q else SB, queries.shape[1]), BF),
            pltpu.SemaphoreType.DMA((count,)),
            pltpu.SemaphoreType.DMA((count,)),
        ],
        compiler_params=pltpu.CompilerParams(vmem_limit_bytes=VMEM),
        cost_estimate=CHEAP,
        name="pack",
    )(selected.T, queries, keys, values)


def inverse(x):
    r = pl.reciprocal(x, approx=True)
    return r * (2.0 - x * r)


def turned(table):
    rows, cols = table.shape
    return jnp.transpose(jnp.concatenate([table, jnp.zeros((LANES - rows, cols), F32)], axis=0))


def pool_body(k_ref, v_ref, pk_ref, pv_ref, gates_ref, out_ref, table_ref):
    step = pl.program_id(0)

    @pl.when(step == 0)
    def _():
        table_ref[...] = turned(jnp.concatenate([gates_ref[b] for b in range(3)], axis=0))

    blocks = k_ref.shape[0] // CB
    for p in range(POOL_PAIRS):
        pair = step * POOL_PAIRS + p
        for ref, pool_ref, start, width in ((k_ref, pk_ref, 0, DK), (v_ref, pv_ref, PK, DV)):
            pool = pool_ref[...]
            lane = lane_of((CB, 2 * width))
            weight = jnp.where(lane < width, column(pool, 2 * pair), column(pool, 2 * pair + 1))
            done = []
            for c in range(blocks):
                rows = ref[c * CB : (c + 1) * CB, p * 2 * width : (p + 1) * 2 * width].astype(F32)
                done.append(jnp.sum(rows * weight, axis=0, keepdims=True))
            first = p * (PK + PV) + start
            out_ref[:, first : first + 2 * width] = jnp.concatenate(done, axis=0).astype(BF)


def pooled(keys, values, pool_keys, pool_values, gates):
    tok, heads = keys.shape[0], keys.shape[1] // DK
    blocks = tok // CB
    return pl.pallas_call(
        pool_body,
        grid=(heads // 2 // POOL_PAIRS,),
        in_specs=[
            pl.BlockSpec((tok, POOL_PAIRS * PK), lambda i: (0, i)),
            pl.BlockSpec((tok, POOL_PAIRS * PV), lambda i: (0, i)),
            pl.BlockSpec((CB, heads), lambda i: (0, 0)),
            pl.BlockSpec((CB, heads), lambda i: (0, 0)),
            pl.BlockSpec((3, heads, tok), lambda i: (0, 0, 0)),
        ],
        out_specs=[
            pl.BlockSpec((blocks, POOL_PAIRS * (PK + PV)), lambda i: (0, i)),
            pl.BlockSpec((tok, LANES), lambda i: (0, 0)),
        ],
        out_shape=[
            jax.ShapeDtypeStruct((blocks, heads * (DK + DV)), BF),
            jax.ShapeDtypeStruct((tok, LANES), F32),
        ],
        compiler_params=pltpu.CompilerParams(vmem_limit_bytes=VMEM),
        cost_estimate=CHEAP,
        name="pool",
    )(keys, values, pool_keys.T, pool_values.T, jnp.transpose(gates, (0, 2, 1)))


def rows_of(window):
    return (window + (UNIT - 2)) // UNIT * UNIT


def cuts(heads):
    full = heads * WIN_MAX
    return (0, full * 3 // 16, full * 3 // 4, full)


def helper_body(win_ref, q_ref, k_ref, v_ref, *rest):
    *parts, out_ref, stat_ref, held, base_ref = rest
    pair = pl.program_id(0)

    @pl.when(pair == 0)
    def _():
        stat_ref[...] = jnp.zeros_like(stat_ref)
        held[...] = jnp.zeros_like(held)
        base_ref[0] = 0

    ones = jnp.ones((WIN_MAX, DV), BF)
    for which in range(2):
        head = 2 * pair + which
        _, b1, b2, _ = gap_biases(win_ref[head])
        q = head_lanes(q_ref[...], which)
        k = k_ref[:, which * LANES : which * LANES + 2 * LANES]
        vext = jnp.concatenate([v_ref[:, which * DV : (which + 1) * DV], ones], axis=1)
        done = []
        for t in range(WIN_MAX // QB):
            rows = slice(t * QB, (t + 1) * QB)
            s = dot_t(q[rows], k[t * QB :])
            s = s + (jnp.concatenate([b2, b1], axis=1) if t == 0 else b2)
            m = jnp.max(s, axis=-1, keepdims=True)
            p = jnp.exp2((s - m) * RATE).astype(BF)
            acc = dot(p, vext[t * QB :])
            total = acc[:, DV:]
            done.append((acc[:, :DV] * inverse(total)).astype(BF))
            stat = m * RATE + jnp.log2(total)
            stat_ref[rows, :] = jnp.where(lane_of(stat.shape) == head, stat, stat_ref[rows, :])
        base = pl.multiple_of(base_ref[0], UNIT)
        held[pl.ds(base, WIN_MAX), :] = jnp.concatenate(done, axis=0)
        base_ref[0] = base + rows_of(win_ref[head])

    @pl.when(pair == pl.num_programs(0) - 1)
    def _():
        out_ref[...] = jnp.transpose(stat_ref[...])[: out_ref.shape[0]]
        at = 0
        for part in parts:
            part[...] = held[at : at + part.shape[0], :]
            at += part.shape[0]


def helper(windows, q_next, keys, values):
    tok, heads = keys.shape[0], keys.shape[1] // DK
    last = tok // WIN_MAX - 1
    ends = cuts(heads)
    shapes = [(stop - start, LANES) for start, stop in zip(ends, ends[1:])]
    whole = lambda shape: pl.BlockSpec(shape, lambda i: (0, 0))
    return pl.pallas_call(
        helper_body,
        grid=(heads // 2,),
        in_specs=[
            pl.BlockSpec(memory_space=pltpu.SMEM),
            pl.BlockSpec((WIN_MAX, PK), lambda i: (0, i)),
            pl.BlockSpec((WIN_MAX, PK), lambda i: (last, i)),
            pl.BlockSpec((WIN_MAX, PV), lambda i: (last, i)),
        ],
        out_specs=[*map(whole, shapes), whole((heads, WIN_MAX))],
        out_shape=[
            *(jax.ShapeDtypeStruct(shape, BF) for shape in shapes),
            jax.ShapeDtypeStruct((heads, WIN_MAX), F32),
        ],
        scratch_shapes=[
            pltpu.VMEM((WIN_MAX, LANES), F32),
            pltpu.VMEM((ends[-1] + WIN_MAX, LANES), BF),
            pltpu.SMEM((1,), jnp.int32),
        ],
        compiler_params=pltpu.CompilerParams(vmem_limit_bytes=VMEM),
        cost_estimate=CHEAP,
        name="helper",
    )(windows, q_next, keys, values)


def local_body(win_ref, q_ref, k_ref, v_ref, table_ref, win_out, own_out, lwin_ref, lown_ref):
    pair = pl.program_id(0)
    heads = 2 * pl.num_programs(0)
    tok = q_ref.shape[0]
    tiles = tok // QB
    pair_rows = 2 * QB
    n_pair = tok // pair_rows

    @pl.when(pair == 0)
    def _():
        lwin_ref[...] = jnp.zeros_like(lwin_ref)
        lown_ref[...] = jnp.zeros_like(lown_ref)

    ones = jnp.ones((tok, DV), BF)
    blank = jnp.zeros((QB, QB), BF)
    for which in range(2):
        head = 2 * pair + which
        b0, b1, b2, bc = gap_biases(win_ref[head])
        lanes = slice(which * LANES, which * LANES + 2 * LANES)
        feat = slice(which * DV, (which + 1) * DV)
        q = head_lanes(q_ref[...], which)
        vext = jnp.concatenate([v_ref[:, feat], ones], axis=1)
        near = [
            dot_t(q[g * pair_rows : (g + 2) * pair_rows], k_ref[g * pair_rows : (g + 1) * pair_rows, lanes])
            for g in range(n_pair)
        ]
        tile = lambda t, u: near[u // 2][(t - u // 2 * 2) * QB : (t - u // 2 * 2 + 1) * QB, u % 2 * QB : (u % 2 + 1) * QB]
        p_near, p_own, tops, tops_o = {}, [], [], []
        for t in range(tiles):
            back = range(max(0, t - 2), t + 1)
            diag = tile(t, t)
            s_w = [(diag if u == t else tile(t, u)) + (b0, b1, b2)[t - u] for u in back]
            m_w = jnp.max(functools.reduce(jnp.maximum, s_w), axis=-1, keepdims=True)
            for u, s in zip(back, s_w):
                p_near[t, u] = jnp.exp2((s - m_w) * RATE).astype(BF)
            s_o = diag + bc
            m_o = jnp.max(s_o, axis=-1, keepdims=True)
            p_own.append(jnp.exp2((s_o - m_o) * RATE).astype(BF))
            tops.append(m_w)
            tops_o.append(m_o)

        acc_w, acc_o = {}, {}
        for g in range(n_pair):
            users = [t for t in range(2 * g, 2 * g + 4) if t < tiles]
            left = [jnp.concatenate([p_near.get((t, 2 * g), blank), p_near.get((t, 2 * g + 1), blank)], axis=1) for t in users]
            left.append(jnp.concatenate([p_own[2 * g], blank], axis=1))
            left.append(jnp.concatenate([blank, p_own[2 * g + 1]], axis=1))
            part = dot(jnp.concatenate(left, axis=0), vext[g * pair_rows : (g + 1) * pair_rows])
            for n, t in enumerate(users):
                one = part[n * QB : (n + 1) * QB]
                acc_w[t] = acc_w[t] + one if t in acc_w else one
            for n in range(2):
                at = (len(users) + n) * QB
                acc_o[2 * g + n] = part[at : at + QB]

        for t in range(tiles):
            rows = slice(t * QB, (t + 1) * QB)
            own, win = acc_o[t], acc_w[t]
            mine = lane_of((QB, LANES)) == head
            own_out[rows, feat] = (own[:, :DV] * inverse(own[:, DV:])).astype(BF)
            lown_ref[rows, :] = jnp.where(mine, tops_o[t] * RATE + jnp.log2(own[:, DV:]), lown_ref[rows, :])
            g2 = column(table_ref[rows, :], 2 * heads + head)
            win_out[rows, feat] = (win[:, :DV] * (g2 * inverse(win[:, DV:]))).astype(BF)
            if t * QB < WIN_MAX:
                lwin_ref[rows, :] = jnp.where(mine, tops[t] * RATE + jnp.log2(win[:, DV:]), lwin_ref[rows, :])


def local(windows, queries, keys, values, table):
    tok, heads = keys.shape[0], keys.shape[1] // DK
    whole = lambda shape: pl.BlockSpec(shape, lambda i: (0,) * len(shape))
    strip = lambda rows, width: pl.BlockSpec((rows, width), lambda i: (0, i))
    return pl.pallas_call(
        local_body,
        grid=(heads // 2,),
        in_specs=[
            pl.BlockSpec(memory_space=pltpu.SMEM),
            strip(tok, PK),
            strip(tok, PK),
            strip(tok, PV),
            whole(table.shape),
        ],
        out_specs=[strip(tok, PV), strip(tok, PV), whole((WIN_MAX, LANES)), whole((tok, LANES))],
        out_shape=[
            jax.ShapeDtypeStruct((tok, heads * DV), BF),
            jax.ShapeDtypeStruct((tok, heads * DV), BF),
            jax.ShapeDtypeStruct((WIN_MAX, LANES), F32),
            jax.ShapeDtypeStruct((tok, LANES), F32),
        ],
        compiler_params=pltpu.CompilerParams(vmem_limit_bytes=VMEM),
        cost_estimate=CHEAP,
        name="local",
    )(windows, queries, keys, values, table)


def far_body(owners, neg_ref, q_ref, win_ref, own_ref, table_ref, bias_ref, stats_ref, lwin_ref, lown_ref, *rest):
    far = owners - 1
    sk, sv, summ_refs = rest[:far], rest[far : 2 * far], rest[2 * far : 2 * far + owners]
    out_ref, a_ref, share_ref = rest[2 * far + owners :]
    pair = pl.program_id(0)
    heads = stats_ref.shape[0]
    tok = q_ref.shape[0]
    n_sel = far * SB

    @pl.when(pair == 0)
    def _():
        lead = turned(stats_ref[...]) + neg_ref[0] - lwin_ref[...]
        less = jnp.exp2(-jnp.abs(lead))
        more = inverse(1.0 + less)
        less = less * more
        share_ref[...] = jnp.where(lead > 0.0, less, more)
        g2 = pltpu.roll(table_ref[:WIN_MAX, :], LANES - 2 * heads, 1)
        a_ref[...] = g2 * jnp.where(lead > 0.0, more, less)

    n_rc = bias_ref.shape[1]
    n_pad = n_rc - n_sel - owners * summ_refs[0].shape[0]
    fill = lambda width: [jnp.zeros((n_pad, width), BF)] if n_pad else []
    krc_pair = jnp.concatenate([r[...] for r in sk] + [r[:, :PK] for r in summ_refs] + fill(PK), axis=0)
    is_sel = lax.broadcasted_iota(jnp.int32, (n_rc, DV), 0) < n_sel
    one_sel = jnp.where(is_sel, 1.0, 0.0).astype(BF)
    one_cmp = jnp.where(is_sel, 0.0, 1.0).astype(BF)
    sel_lane = lane_of((QB, LANES)) < n_sel % LANES

    for which in range(2):
        head = 2 * pair + which
        lanes = slice(which * LANES, which * LANES + 2 * LANES)
        feat = slice(which * DV, (which + 1) * DV)
        q = head_lanes(q_ref[...], which)
        v_sel = [r[:, feat] for r in sv]
        v_cmp = [r[:, PK + which * DV : PK + (which + 1) * DV] for r in summ_refs] + fill(DV)
        zero = lambda n: [jnp.zeros((n, DV), BF)]
        wrc = jnp.concatenate(
            [
                jnp.concatenate(v_sel + zero(n_rc - n_sel), axis=0),
                jnp.concatenate(zero(n_sel) + v_cmp, axis=0),
                one_sel,
                one_cmp,
            ],
            axis=1,
        )
        s_rc = dot_t(q, krc_pair[:, lanes])
        p_far, keep, sink = [], [], []
        for t in range(tok // QB):
            rows = slice(t * QB, (t + 1) * QB)
            x = s_rc[rows] + bias_ref[rows, :]
            pieces = [(x[:, n : n + LANES], n) for n in range(0, n_rc, LANES)]
            sel_side, cmp_side = [], []
            for piece, n in pieces:
                if n < n_sel:
                    sel_side.append(piece if n + LANES <= n_sel else jnp.where(sel_lane, piece, NEG))
                if n + LANES > n_sel:
                    cmp_side.append(piece if n >= n_sel else jnp.where(sel_lane, NEG, piece))
            here = column(lown_ref[rows, :], head)
            m_s = jnp.maximum(jnp.max(functools.reduce(jnp.maximum, sel_side), axis=-1, keepdims=True) * RATE, here)
            m_c = jnp.maximum(jnp.max(functools.reduce(jnp.maximum, cmp_side), axis=-1, keepdims=True) * RATE, 0.0)
            p_rc = []
            for piece, n in pieces:
                top = m_s if n + LANES <= n_sel else m_c if n >= n_sel else jnp.where(sel_lane, m_s, m_c)
                p_rc.append(jnp.exp2(piece * RATE - top).astype(BF))
            p_far.append(jnp.concatenate(p_rc, axis=1))
            keep.append(jnp.exp2(here - m_s))
            sink.append(jnp.exp2(-m_c))

        acc = dot(jnp.concatenate(p_far, axis=0), wrc)
        for t in range(tok // QB):
            rows = slice(t * QB, (t + 1) * QB)
            rc = acc[rows]
            g0, g1 = (column(table_ref[rows, :], b * heads + head) for b in range(2))
            own = own_ref[rows, feat].astype(F32) * keep[t]
            sel = (own + rc[:, :DV]) * (g1 * inverse(keep[t] + rc[:, 2 * DV : 3 * DV]))
            summ = rc[:, DV : 2 * DV] * (g0 * inverse(rc[:, 3 * DV :] + sink[t]))
            win = win_ref[rows, feat].astype(F32)
            if t * QB < WIN_MAX:
                win = win * column(share_ref[rows, :], head)
            out_ref[rows, feat] = (summ + sel + win).astype(BF)


def far(neg, queries, win, own, table, bias, stats, lwin, lown, far_kv, summ):
    tok, heads = queries.shape[0], queries.shape[1] // DK
    owners = len(summ)
    n_sum = summ[0].shape[0]
    skip = heads * DK // PV
    whole = lambda shape: pl.BlockSpec(shape, lambda i: (0,) * len(shape))
    strip = lambda rows, width, skip=0: pl.BlockSpec((rows, width), lambda i: (0, i + skip))
    return pl.pallas_call(
        functools.partial(far_body, owners),
        grid=(heads // 2,),
        in_specs=[pl.BlockSpec(memory_space=pltpu.SMEM), strip(tok, PK), strip(tok, PV), strip(tok, PV)]
        + [whole(one.shape) for one in (table, bias, stats, lwin, lown)]
        + [strip(SB, PK)] * len(far_kv)
        + [strip(SB, PV, skip)] * len(far_kv)
        + [strip(n_sum, PK + PV)] * owners,
        out_specs=[strip(tok, PV), whole((WIN_MAX, LANES))],
        out_shape=[
            jax.ShapeDtypeStruct((tok, heads * DV), BF),
            jax.ShapeDtypeStruct((WIN_MAX, LANES), F32),
        ],
        scratch_shapes=[pltpu.VMEM((WIN_MAX, LANES), F32)],
        compiler_params=pltpu.CompilerParams(vmem_limit_bytes=VMEM),
        cost_estimate=pl.CostEstimate(flops=heads * tok * 2_000_000, bytes_accessed=24 << 20, transcendentals=0),
        name="far",
    )(neg, queries, win, own, table, bias, stats, lwin, lown, *far_kv, *far_kv, *summ)


def merge_body(count, win_ref, a_ref, base_ref, *rest):
    parts, (out_ref, held, table, weight_ref, sem_in, sem_row, sem_out) = rest[:count], rest[count:]
    heads = win_ref.shape[0]
    arrive, at = [pltpu.make_async_copy(a_ref, weight_ref, sem_in.at[count])], 0
    for n, part in enumerate(parts):
        arrive.append(pltpu.make_async_copy(part, held.at[pl.ds(at, part.shape[0])], sem_in.at[n]))
        at += part.shape[0]
    strips = [pl.ds(r, MERGE_ROWS) for r in range(0, WIN_MAX, MERGE_ROWS)]
    inward = [pltpu.make_async_copy(base_ref.at[r], table.at[r], sem_row.at[n]) for n, r in enumerate(strips)]
    outward = [pltpu.make_async_copy(table.at[r], out_ref.at[r], sem_out.at[n]) for n, r in enumerate(strips)]
    for copy in arrive + inward:
        copy.start()
    held[at:, :] = jnp.zeros((held.shape[0] - at, LANES), BF)
    for copy in arrive:
        copy.wait()
    for n in range(len(strips)):
        inward[n].wait()
        first = n * MERGE_ROWS
        rows = slice(first, first + MERGE_ROWS)
        base = jnp.int32(first)
        for h in range(heads):
            feat = slice(h * DV, (h + 1) * DV)
            away = held[pl.ds(pl.multiple_of(base, UNIT), MERGE_ROWS), :].astype(F32)
            table[rows, feat] = (table[rows, feat].astype(F32) + weight_ref[rows, h : h + 1] * away).astype(BF)
            base = base + rows_of(win_ref[h])
        outward[n].start()
    for copy in outward:
        copy.wait()


def merge(windows, weight, base, parts):
    heads, width = windows.shape[0], base.shape[1]
    anywhere = pl.BlockSpec(memory_space=pl.ANY)
    strips = WIN_MAX // MERGE_ROWS
    return pl.pallas_call(
        functools.partial(merge_body, len(parts)),
        in_specs=[pl.BlockSpec(memory_space=pltpu.SMEM)] + [anywhere] * (2 + len(parts)),
        out_specs=anywhere,
        out_shape=jax.ShapeDtypeStruct(base.shape, base.dtype),
        input_output_aliases={2: 0},
        scratch_shapes=[
            pltpu.VMEM((heads * WIN_MAX + WIN_MAX, LANES), BF),
            pltpu.VMEM((WIN_MAX, width), BF),
            pltpu.VMEM((WIN_MAX, LANES), F32),
            pltpu.SemaphoreType.DMA((len(parts) + 1,)),
            pltpu.SemaphoreType.DMA((strips,)),
            pltpu.SemaphoreType.DMA((strips,)),
        ],
        compiler_params=pltpu.CompilerParams(vmem_limit_bytes=VMEM),
        cost_estimate=CHEAP,
        name="merge",
    )(windows, weight, base, *parts)


def shards(queries, keys, values, gates, pool_keys, pool_values, windows, selected):
    tok = queries.shape[0]
    heads = queries.shape[1] // DK
    owners = lax.axis_size("seq")
    rank = lax.axis_index("seq")
    q_here = tok // QB
    per_owner = tok // SB

    steps = tuple(range(1, owners))
    (first,) = pack(steps[:1], 0, owners, selected, queries, keys, values)
    far_kv = [passed_along(first, "seq", 1)]
    keys_after, _ = lax.optimization_barrier((keys, first))
    *sends, q_first = pack(steps[1:], 1, owners, selected, queries, keys_after, values)
    q_next = passed_along(q_first, "seq", -1)
    keys_after, _ = lax.optimization_barrier((keys, q_first))
    mine, table = pooled(keys_after, values, pool_keys, pool_values, gates)
    win, own, lwin, lown = local(windows, queries, keys_after, values, table)
    mine, far_kv[0], win = lax.optimization_barrier((mine, far_kv[0], win))
    summ = [mine, passed_along(mine, "seq", 1)]
    for d in steps[1:]:
        summ.append(passed_along(summ[-1], "seq", 1, d - 1))
    sends[0], _ = lax.optimization_barrier((sends[0], summ[2]))
    far_kv += [passed_along(send, "seq", d + 2) for d, send in enumerate(sends)]

    owner_of = jnp.where(selected >= 0, selected // per_owner, -1)
    lists = lax.dynamic_slice_in_dim(owner_of, rank * q_here, q_here, 0)
    back = jnp.arange(1, owners, dtype=jnp.int32)
    named = jnp.any(lists[:, :, None] == (rank - back)[None, None, :], axis=1) & (rank >= back)[None, :]
    named = jnp.repeat(jnp.repeat(named, QB, axis=0), SB, axis=1)
    n_own = tok // CB
    slot = jnp.arange(owners * n_own, dtype=jnp.int32)
    block = (rank - slot // n_own) * n_own + slot % n_own
    pos = rank * tok + jnp.arange(tok, dtype=jnp.int32)
    ended = (block >= 0)[None, :] & ((block * CB + CB - 1)[None, :] <= pos[:, None])
    live = jnp.concatenate([named, ended], axis=1)
    live = jnp.pad(live, ((0, 0), (0, -live.shape[1] % LANES)))
    bias = jnp.where(live, 0.0, NEG).astype(F32)

    neg = jnp.where(rank == 0, NEG, 0.0).astype(F32).reshape(1)
    needed = lax.pmax(jnp.sum(rows_of(windows)), ("head", "sub"))
    q_next, summ[-1], needed, bias, neg = lax.optimization_barrier((q_next, summ[-1], needed, bias, neg))
    early, away, spare, stats = helper(windows, q_next, keys, values)
    stats = passed_along(stats, "seq", 1)
    early = passed_along(early, "seq", 1)
    away, far_kv, summ, stats = lax.optimization_barrier((away, far_kv, summ, stats))
    away = passed_along(away, "seq", 1)
    early, win = lax.optimization_barrier((early, win))

    out, weight = far(neg, queries, win, own, table, bias, stats, lwin, lown, far_kv, summ)
    spare, weight = lax.optimization_barrier((spare, weight))
    spare = lax.cond(
        needed > cuts(heads)[-2],
        lambda rows: passed_along(rows, "seq", 1),
        jnp.zeros_like,
        spare,
    )
    return merge(windows, weight, out, [early, away, spare])


def solution(mesh):
    placed = (
        P(("parts", "seq"), ("head", "sub")),
        P(("parts", "seq"), ("head", "sub")),
        P(("parts", "seq"), ("head", "sub")),
        P(None, ("parts", "seq"), ("head", "sub")),
        P(("head", "sub"), None),
        P(("head", "sub"), None),
        P(("head", "sub")),
        P("parts", None),
    )
    return jax.shard_map(
        shards,
        mesh=mesh,
        in_specs=placed,
        out_specs=P(("parts", "seq"), ("head", "sub")),
        check_vma=False,
    )
```

profile of v0, /device:TPU:0, one launch (start us, length us, event | category | flops | bytes accessed | tf_op | source)
XLA Modules:
  0.0 182.0 jit_solution(17536363833215209954)
XLA Ops:
  0.0 3.2 %pack.2 = bf16[64,10240]{1,0:T(8,128)(2,1)} custom-call(s32[8,16]{1,0:T(8,128)} %bitcast.17, bf16[512,6144]{1,0:T(8,128)(2,1)} %q_ref.7, bf16[512,6144]{1,0:T(8,128)(2,1)} %k_ref.6, bf16[512,4096]{1,0:T(8,128)(2,1)} %v_ref.9), custom_call_target="tpu_custom_call" | custom-call | flops 1 | bytes 1 | tf_op jit(solution)/shard_map/pack/pallas_call | solution.py:111
  3.2 0.0 copy-start.4
  3.2 0.0 copy-start.5
  3.2 6.1 %collective-permute-start.2 = (bf16[64,10240]{1,0:T(8,128)(2,1)}, bf16[64,10240]{1,0:T(8,128)(2,1)}, u32[]{:S(2)}, u32[]{:S(2)}) collective-permute-start(bf16[64,10240]{1,0:T(8,128)(2,1)} %pack.2), channel_id=1, source_target_pairs={{0,4},{4,8},{8,12},{1,5},{5,9},{9,13},{2,6},{6,10},{10,14},{3,7},{... | collective-permute-start | bytes 3932168 | tf_op jit(solution)/shard_map/ppermute | solution.py:35
  9.3 5.7 %pack.3 = (bf16[64,10240]{1,0:T(8,128)(2,1)}, bf16[64,10240]{1,0:T(8,128)(2,1)}, bf16[256,6144]{1,0:T(8,128)(2,1)}) custom-call(s32[8,16]{1,0:T(8,128)} %bitcast.18, bf16[512,6144]{1,0:T(8,128)(2,1)} %q_ref.7, bf16[512,6144]{1,0:T(8,128)(2,1)} %k_ref.6, bf16[512,4096]{1,0:T(8,128)(2,1)} %v_ref.9), custom_call_target="tpu_custom_call" | custom-call | flops 1 | bytes 1 | tf_op jit(solution)/shard_map/pack/pallas_call | solution.py:111
  15.0 1.3 collective-permute-start.1
  16.3 6.6 %collective-permute-start.8 = (bf16[64,10240]{1,0:T(8,128)(2,1)}, bf16[64,10240]{1,0:T(8,128)(2,1)}, u32[]{:S(2)}, u32[]{:S(2)}) collective-permute-start(bf16[64,10240]{1,0:T(8,128)(2,1)} %get-tuple-element.67), channel_id=1, source_target_pairs={{0,12},{1,13},{2,14},{3,15},{16,28},{17,29},{18,30},{19,31}} | collective-permute-start | bytes 3932168 | tf_op jit(solution)/shard_map/ppermute | solution.py:35
  22.9 0.7 copy.17
  23.6 0.7 copy.18
  24.3 8.8 %pool.1 = (bf16[16,10240]{1,0:T(8,128)(2,1)}, f32[512,128]{1,0:T(8,128)}) custom-call(bf16[512,6144]{1,0:T(8,128)(2,1)} %k_ref.6, bf16[512,4096]{1,0:T(8,128)(2,1)} %v_ref.9, f32[32,32]{1,0:T(8,128)} %bitcast.15, f32[32,32]{1,0:T(8,128)} %bitcast.16, f32[3,32,512]{2,1,0:T(8,128)} %bitcast.14), custom_call_target="tpu_custom_call" | custom-call | flops 1 | bytes 1 | tf_op jit(solution)/shard_map/pool/pallas_call | solution.py:163
  33.1 0.0 copy-start.6
  33.1 21.1 %local.1 = (bf16[512,4096]{1,0:T(8,128)(2,1)}, bf16[512,4096]{1,0:T(8,128)(2,1)}, f32[256,128]{1,0:T(8,128)}, f32[512,128]{1,0:T(8,128)}) custom-call(s32[32]{0:T(128)} %win_ref.5, bf16[512,6144]{1,0:T(8,128)(2,1)} %q_ref.7, bf16[512,6144]{1,0:T(8,128)(2,1)} %k_ref.6, bf16[512,4096]{1,0:T(8,128)(2,1)} %v_ref.9, f32[512,128]{1,0:T(8,128)} %get-tuple-element.52.table_ref), custom_call_target="tpu_custom_call" | custom-call | flops 1 | bytes 1 | tf_op jit(solution)/shard_map/local/pallas_call | solution.py:340
  54.2 0.0 collective-permute-done.2.rest_0_.rest_3_
  54.2 2.0 %collective-permute-start.3 = (bf16[16,10240]{1,0:T(8,128)(2,1)S(1)}, bf16[16,10240]{1,0:T(8,128)(2,1)}, u32[]{:S(2)}, u32[]{:S(2)}) collective-permute-start(bf16[16,10240]{1,0:T(8,128)(2,1)S(1)} %copy-done.8), channel_id=1, source_target_pairs={{0,4},{4,8},{8,12},{1,5},{5,9},{9,13},{2,6},{6,10},{10,14},{3,7},{... | collective-permute-start | bytes 983048 | tf_op jit(solution)/shard_map/ppermute | solution.py:35
  56.3 0.1 constant_dynamic-slice_fusion
  56.3 0.1 copy.19
  56.4 15.1 %collective-permute-done.3.rest_7_ = bf16[16,10240]{1,0:T(8,128)(2,1)} collective-permute-done((bf16[16,10240]{1,0:T(8,128)(2,1)S(1)}, bf16[16,10240]{1,0:T(8,128)(2,1)}, u32[]{:S(2)}, u32[]{:S(2)}) %collective-permute-start.3) | collective-permute-done | bytes 327712 | tf_op jit(solution)/shard_map/ppermute | solution.py:35
  71.5 0.7 collective-permute-start.4
  72.2 0.2 compare_reduce_fusion
  72.4 0.7 multiply_reduce_fusion
  73.1 0.0 collective-permute-done.4.rest_8_
  73.2 0.7 copy-done.9
  73.9 15.0 %collective-permute-start.7 = (bf16[64,10240]{1,0:T(8,128)(2,1)}, bf16[64,10240]{1,0:T(8,128)(2,1)}, u32[]{:S(2)}, u32[]{:S(2)}) collective-permute-start(bf16[64,10240]{1,0:T(8,128)(2,1)} %get-tuple-element.66), channel_id=1, source_target_pairs={{0,8},{4,12},{1,9},{5,13},{2,10},{6,14},{3,11},{7,15},{16,24},{20,... | collective-permute-start | bytes 3932168 | tf_op jit(solution)/shard_map/ppermute | solution.py:35
  88.9 0.1 broadcast_and_fusion
  89.0 5.6 %pmax.7 = s32[]{:T(128)} all-reduce(s32[]{:T(128)} %multiply_reduce_fusion), channel_id=1, replica_groups=mesh['parts'=2,'seq'=4,'head'=2,'sub'=2] {'head','sub'}, use_global_device_ids=true, to_apply=%region_1.2 | all-reduce | flops 1 | bytes 8 | tf_op jit(solution)/shard_map/pmax | solution.py:565
  94.6 0.1 broadcast_bitcast_fusion
  94.7 0.3 copy.20
  95.0 0.7 collective-permute-start.5
  95.7 0.1 compare_and_fusion
  95.9 1.0 add_select_fusion.bias_ref
  96.8 0.0 collective-permute-done.5.rest_9_
  96.8 0.0 collective-permute-done.1.q_ref
  96.8 0.7 copy-done.10
  97.6 1.7 copy-done
  99.2 19.7 %helper.1 = (bf16[1536,128]{1,0:T(8,128)(2,1)}, bf16[4608,128]{1,0:T(8,128)(2,1)}, bf16[2048,128]{1,0:T(8,128)(2,1)}, f32[32,256]{1,0:T(8,128)}) custom-call(s32[32]{0:T(128)} %win_ref.5, bf16[256,6144]{1,0:T(8,128)(2,1)} %copy-done, bf16[512,6144]{1,0:T(8,128)(2,1)} %k_ref.6, bf16[512,4096]{1,0:T(8,128)(2,1)} %v_ref.9), custom_call_target="tpu_custom_call" | custom-call | flops 1 | bytes 1 | tf_op jit(solution)/shard_map/helper/pallas_call | solution.py:244
  119.0 3.6 %collective-permute-start.6 = (bf16[1536,128]{1,0:T(8,128)(2,1)}, bf16[1536,128]{1,0:T(8,128)(2,1)S(1)}, u32[]{:S(2)}, u32[]{:S(2)}) collective-permute-start(bf16[1536,128]{1,0:T(8,128)(2,1)} %get-tuple-element.58), channel_id=1, source_target_pairs={{0,4},{4,8},{8,12},{1,5},{5,9},{9,13},{2,6},{6,10},{10,14},{3,7},{... | collective-permute-start | bytes 1179656 | tf_op jit(solution)/shard_map/ppermute | solution.py:35
  122.6 7.5 %collective-permute-start.9 = (f32[32,256]{1,0:T(8,128)}, f32[32,256]{1,0:T(8,128)S(1)}, u32[]{:S(2)}, u32[]{:S(2)}) collective-permute-start(f32[32,256]{1,0:T(8,128)} %get-tuple-element.69), channel_id=1, source_target_pairs={{0,4},{4,8},{8,12},{1,5},{5,9},{9,13},{2,6},{6,10},{10,14},{3,7},{... | collective-permute-start | bytes 98312 | tf_op jit(solution)/shard_map/ppermute | solution.py:35
  130.7 0.0 collective-permute-done.8.rest_2_.rest_5_
  130.8 1.2 collective-permute-done.9.stats_ref
  132.0 0.0 collective-permute-done.7.rest_1_.rest_4_
  132.0 19.4 %collective-permute-start.10 = (bf16[4608,128]{1,0:T(8,128)(2,1)}, bf16[4608,128]{1,0:T(8,128)(2,1)S(1)}, u32[]{:S(2)}, u32[]{:S(2)}) collective-permute-start(bf16[4608,128]{1,0:T(8,128)(2,1)} %get-tuple-element.84), channel_id=1, source_target_pairs={{0,4},{4,8},{8,12},{1,5},{5,9},{9,13},{2,6},{6,10},{10,14},{3,7},{... | collective-permute-start | bytes 3538952 | tf_op jit(solution)/shard_map/ppermute | solution.py:35
  151.4 0.0 collective-permute-done.6.rest_0_
  151.4 22.7 %far.1 = (bf16[512,4096]{1,0:T(8,128)(2,1)}, f32[256,128]{1,0:T(8,128)}) custom-call(f32[1]{0:T(128)} %bitcast.5.neg_ref, bf16[512,6144]{1,0:T(8,128)(2,1)} %q_ref.7, bf16[512,4096]{1,0:T(8,128)(2,1)} %get-tuple-element.60.win_ref, bf16[512,4096]{1,0:T(8,128)(2,1)} %get-tuple-element.61.own_ref, f32[512,128]{1,0:T(8,128)} %get-tuple-element.52.table_ref, ...), custom_call_target="tpu_custom_call" | custom-call | flops 32768000000 | bytes 25165824 | tf_op jit(solution)/shard_map/far/pallas_call | solution.py:452
  174.1 0.9 conditional.1
  174.1 0.9 broadcast.151
  174.9 1.0 collective-permute-done.10.rest_1_
  175.9 1.0 copy-done.1
  177.0 5.0 %merge.1 = bf16[512,4096]{1,0:T(8,128)(2,1)} custom-call(s32[32]{0:T(128)} %win_ref.5, f32[256,128]{1,0:T(8,128)} %get-tuple-element.81.a_ref, bf16[512,4096]{1,0:T(8,128)(2,1)} %get-tuple-element.82.base_ref, bf16[1536,128]{1,0:T(8,128)(2,1)} %copy-done.2, bf16[4608,128]{1,0:T(8,128)(2,1)} %copy-done.1, ...), custom_call_target="tpu_custom_call", output_to_operand_aliasing={{}: (2, {})} | custom-call | flops 1 | bytes 1 | tf_op jit(solution)/shard_map/merge/pallas_call | solution.py:506
  (25 shorter events, 0.1 us)
Async XLA Ops:
  3.2 19.8 %copy-start.4 = (f32[32,32]{1,0:T(8,128)S(1)}, f32[32,32]{1,0:T(8,128)}, u32[]{:S(2)}) copy-start(f32[32,32]{1,0:T(8,128)} %param.14) | copy-start | bytes 12292
  3.2 20.4 %copy-start.5 = (f32[32,32]{1,0:T(8,128)S(1)}, f32[32,32]{1,0:T(8,128)}, u32[]{:S(2)}) copy-start(f32[32,32]{1,0:T(8,128)} %param.15) | copy-start | bytes 12292
  3.2 51.0 %collective-permute-start.2 = (bf16[64,10240]{1,0:T(8,128)(2,1)}, bf16[64,10240]{1,0:T(8,128)(2,1)}, u32[]{:S(2)}, u32[]{:S(2)}) collective-permute-start(bf16[64,10240]{1,0:T(8,128)(2,1)} %pack.2), channel_id=1, source_target_pairs={{0,4},{4,8},{8,12},{1,5},{5,9},{9,13},{2,6},{6,10},{10,14},{3,7},{... | collective-permute-start | bytes 3932168 | tf_op jit(solution)/shard_map/ppermute | solution.py:35
  15.0 81.8 %collective-permute-start.1 = (bf16[256,6144]{1,0:T(8,128)(2,1)}, bf16[256,6144]{1,0:T(8,128)(2,1)S(1)}, u32[]{:S(2)}, u32[]{:S(2)}) collective-permute-start(bf16[256,6144]{1,0:T(8,128)(2,1)} %get-tuple-element.49), channel_id=1, source_target_pairs={{4,0},{8,4},{12,8},{5,1},{9,5},{13,9},{6,2},{10,6},{14,10},{7,3},{... | collective-permute-start | bytes 9437192 | tf_op jit(solution)/shard_map/ppermute | solution.py:35
  16.3 114.4 %collective-permute-start.8 = (bf16[64,10240]{1,0:T(8,128)(2,1)}, bf16[64,10240]{1,0:T(8,128)(2,1)}, u32[]{:S(2)}, u32[]{:S(2)}) collective-permute-start(bf16[64,10240]{1,0:T(8,128)(2,1)} %get-tuple-element.67), channel_id=1, source_target_pairs={{0,12},{1,13},{2,14},{3,15},{16,28},{17,29},{18,30},{19,31}} | collective-permute-start | bytes 3932168 | tf_op jit(solution)/shard_map/ppermute | solution.py:35
  33.1 21.1 %copy-start.8 = (bf16[16,10240]{1,0:T(8,128)(2,1)S(1)}, bf16[16,10240]{1,0:T(8,128)(2,1)}, u32[]{:S(2)}) copy-start(bf16[16,10240]{1,0:T(8,128)(2,1)} %get-tuple-element.76.rest_6_) | copy-start | bytes 983044
  33.1 23.2 %copy-start.3 = (s32[16,8]{0,1:T(8,128)S(1)}, s32[16,8]{0,1:T(8,128)}, u32[]{:S(2)}) copy-start(s32[16,8]{0,1:T(8,128)} %param.17) | copy-start | bytes 1540
  33.1 39.4 %copy-start.6 = (s32[32]{0:T(128)S(1)}, s32[32]{0:T(128)}, u32[]{:S(2)}) copy-start(s32[32]{0:T(128)} %win_ref.5) | copy-start | bytes 388
  54.2 17.3 %collective-permute-start.3 = (bf16[16,10240]{1,0:T(8,128)(2,1)S(1)}, bf16[16,10240]{1,0:T(8,128)(2,1)}, u32[]{:S(2)}, u32[]{:S(2)}) collective-permute-start(bf16[16,10240]{1,0:T(8,128)(2,1)S(1)} %copy-done.8), channel_id=1, source_target_pairs={{0,4},{4,8},{8,12},{1,5},{5,9},{9,13},{2,6},{6,10},{10,14},{3,7},{... | collective-permute-start | bytes 983048 | tf_op jit(solution)/shard_map/ppermute | solution.py:35
  71.5 1.6 collective-permute-start.4
  73.2 0.7 copy-start.9
  73.9 58.1 %collective-permute-start.7 = (bf16[64,10240]{1,0:T(8,128)(2,1)}, bf16[64,10240]{1,0:T(8,128)(2,1)}, u32[]{:S(2)}, u32[]{:S(2)}) collective-permute-start(bf16[64,10240]{1,0:T(8,128)(2,1)} %get-tuple-element.66), channel_id=1, source_target_pairs={{0,8},{4,12},{1,9},{5,13},{2,10},{6,14},{3,11},{7,15},{16,24},{20,... | collective-permute-start | bytes 3932168 | tf_op jit(solution)/shard_map/ppermute | solution.py:35
  95.0 1.8 collective-permute-start.5
  96.8 0.7 copy-start.10
  97.6 1.7 copy-start
  119.0 32.4 %collective-permute-start.6 = (bf16[1536,128]{1,0:T(8,128)(2,1)}, bf16[1536,128]{1,0:T(8,128)(2,1)S(1)}, u32[]{:S(2)}, u32[]{:S(2)}) collective-permute-start(bf16[1536,128]{1,0:T(8,128)(2,1)} %get-tuple-element.58), channel_id=1, source_target_pairs={{0,4},{4,8},{8,12},{1,5},{5,9},{9,13},{2,6},{6,10},{10,14},{3,7},{... | collective-permute-start | bytes 1179656 | tf_op jit(solution)/shard_map/ppermute | solution.py:35
  122.6 9.4 %collective-permute-start.9 = (f32[32,256]{1,0:T(8,128)}, f32[32,256]{1,0:T(8,128)S(1)}, u32[]{:S(2)}, u32[]{:S(2)}) collective-permute-start(f32[32,256]{1,0:T(8,128)} %get-tuple-element.69), channel_id=1, source_target_pairs={{0,4},{4,8},{8,12},{1,5},{5,9},{9,13},{2,6},{6,10},{10,14},{3,7},{... | collective-permute-start | bytes 98312 | tf_op jit(solution)/shard_map/ppermute | solution.py:35
  132.0 19.4 %copy-start.11 = (f32[32,256]{1,0:T(8,128)}, f32[32,256]{1,0:T(8,128)S(1)}, u32[]{:S(2)}) copy-start(f32[32,256]{1,0:T(8,128)S(1)} %collective-permute-done.9.stats_ref) | copy-start | bytes 98308
  132.0 44.0 %collective-permute-start.10 = (bf16[4608,128]{1,0:T(8,128)(2,1)}, bf16[4608,128]{1,0:T(8,128)(2,1)S(1)}, u32[]{:S(2)}, u32[]{:S(2)}) collective-permute-start(bf16[4608,128]{1,0:T(8,128)(2,1)} %get-tuple-element.84), channel_id=1, source_target_pairs={{0,4},{4,8},{8,12},{1,5},{5,9},{9,13},{2,6},{6,10},{10,14},{3,7},{... | collective-permute-start | bytes 3538952 | tf_op jit(solution)/shard_map/ppermute | solution.py:35
  151.4 22.7 %copy-start.2 = (bf16[1536,128]{1,0:T(8,128)(2,1)}, bf16[1536,128]{1,0:T(8,128)(2,1)S(1)}, u32[]{:S(2)}) copy-start(bf16[1536,128]{1,0:T(8,128)(2,1)S(1)} %collective-permute-done.6.rest_0_) | copy-start | bytes 1179652
  151.4 22.7 %copy-start.7 = (bf16[2048,128]{1,0:T(8,128)(2,1)S(1)}, bf16[2048,128]{1,0:T(8,128)(2,1)}, u32[]{:S(2)}) copy-start(bf16[2048,128]{1,0:T(8,128)(2,1)} %get-tuple-element.86) | copy-start | bytes 1572868
  175.9 1.0 copy-start.1
where the time goes:
time: 185 us; the launch traced here: 182 us
  Pallas kernels  86.2 us (47%)
  starting transfers between devices  62.9 us (34%)
  waiting for transfers between devices  17.3 us (9%)
  local copies, waits for them, and re-layouts  6.97 us (4%)
  blocking collectives  5.61 us (3%)
  other arithmetic  2.14 us (1%)
    ppermute x10, starting transfers between devices, passed_along(): lax.ppermute(value, axis, [(source, source + steps) for source in range(l...  62.9 us
    pallas_call x1, Pallas kernels, far(): pl.pallas_call(functools.partial(far_body, owners), grid=(heads // 2,), i...  22.7 us
    pallas_call x1, Pallas kernels, local(): pl.pallas_call(local_body, grid=(heads // 2,), in_specs=[pl.BlockSpec(mem...  21.1 us
    pallas_call x1, Pallas kernels, helper(): pl.pallas_call(helper_body, grid=(heads // 2,), in_specs=[pl.BlockSpec(me...  19.7 us
    ppermute x10, waiting for transfers between devices, passed_along(): lax.ppermute(value, axis, [(source, source + steps) for source in range(l...  17.3 us
    pallas_call x2, Pallas kernels, pack(): pl.pallas_call(functools.partial(pack_body, steps, with_q, owners), in_sp...  8.88 us
    pallas_call x1, Pallas kernels, pooled(): pl.pallas_call(pool_body, grid=(heads // 2 // POOL_PAIRS,), in_specs=[pl....  8.78 us
    unnamed x28, local copies, waits for them, and re-layouts  5.65 us
  transfers between devices with their start and end apart: 10, of which 3 were waited for; matrix products, arithmetic and copies ran while one was open for 3% of the time, Pallas kernels for 43%

commit v1 on v0

--- a/solution.py
+++ b/solution.py
@@ -517,7 +517,7 @@
             pltpu.SemaphoreType.DMA((strips,)),
             pltpu.SemaphoreType.DMA((strips,)),
         ],
-        compiler_params=pltpu.CompilerParams(vmem_limit_bytes=VMEM),
+        compiler_params=pltpu.CompilerParams(vmem_limit_bytes=VMEM // 2),
         cost_estimate=CHEAP,
         name="merge",
     )(windows, weight, base, *parts)

time: 185 us -> 183 us (0.989)
  local copies, waits for them, and re-layouts: 6.97 us -> 4.46 us
  starting transfers between devices: 62.9 us -> 65 us
    unnamed x28 -> x30, local copies, waits for them, and re-layouts: 5.65 us -> 3.13 us
    ppermute x10, starting transfers between devices: 62.9 us -> 65 us  [passed_along(): lax.ppermute(value, axis, [(source, source + steps) for source in range(l...]
where the time goes in v1:
time: 183 us; the launch traced here: 181 us
  Pallas kernels  86 us (47%)
  starting transfers between devices  65 us (36%)
  waiting for transfers between devices  16.6 us (9%)
  blocking collectives  5.61 us (3%)
  local copies, waits for them, and re-layouts  4.46 us (2%)
  other arithmetic  2.14 us (1%)
    ppermute x10, starting transfers between devices, passed_along(): lax.ppermute(value, axis, [(source, source + steps) for source in range(l...  65 us
    pallas_call x1, Pallas kernels, far(): pl.pallas_call(functools.partial(far_body, owners), grid=(heads // 2,), i...  22.5 us
    pallas_call x1, Pallas kernels, local(): pl.pallas_call(local_body, grid=(heads // 2,), in_specs=[pl.BlockSpec(mem...  21.2 us
    pallas_call x1, Pallas kernels, helper(): pl.pallas_call(helper_body, grid=(heads // 2,), in_specs=[pl.BlockSpec(me...  19.5 us
    ppermute x10, waiting for transfers between devices, passed_along(): lax.ppermute(value, axis, [(source, source + steps) for source in range(l...  16.6 us
    pallas_call x2, Pallas kernels, pack(): pl.pallas_call(functools.partial(pack_body, steps, with_q, owners), in_sp...  9.02 us
    pallas_call x1, Pallas kernels, pooled(): pl.pallas_call(pool_body, grid=(heads // 2 // POOL_PAIRS,), in_specs=[pl....  8.77 us
    pmax x1, blocking collectives, shards(): needed = lax.pmax(jnp.sum(rows_of(windows)), ('head', 'sub'))  5.61 us
  transfers between devices with their start and end apart: 10, of which 3 were waited for; matrix products, arithmetic and copies ran while one was open for 3% of the time, Pallas kernels for 43%

profile of v1, /device:TPU:0, one launch (start us, length us, event | category | flops | bytes accessed | tf_op | source)
XLA Modules:
  0.0 180.7 jit_solution(14611123973969711957)
XLA Ops:
  0.0 3.1 %pack.2 = bf16[64,10240]{1,0:T(8,128)(2,1)} custom-call(s32[8,16]{1,0:T(8,128)} %bitcast.17, bf16[512,6144]{1,0:T(8,128)(2,1)} %q_ref.7, bf16[512,6144]{1,0:T(8,128)(2,1)} %k_ref.6, bf16[512,4096]{1,0:T(8,128)(2,1)} %v_ref.9), custom_call_target="tpu_custom_call" | custom-call | flops 1 | bytes 1 | tf_op jit(solution)/shard_map/pack/pallas_call | solution.py:111
  3.1 0.0 copy-start.4
  3.1 0.0 copy-start.5
  3.1 5.0 %collective-permute-start.2 = (bf16[64,10240]{1,0:T(8,128)(2,1)}, bf16[64,10240]{1,0:T(8,128)(2,1)S(1)}, u32[]{:S(2)}, u32[]{:S(2)}) collective-permute-start(bf16[64,10240]{1,0:T(8,128)(2,1)} %pack.2), channel_id=1, source_target_pairs={{0,4},{4,8},{8,12},{1,5},{5,9},{9,13},{2,6},{6,10},{10,14},{3,7},{... | collective-permute-start | bytes 3932168 | tf_op jit(solution)/shard_map/ppermute | solution.py:35
  8.1 5.9 %pack.3 = (bf16[64,10240]{1,0:T(8,128)(2,1)}, bf16[64,10240]{1,0:T(8,128)(2,1)}, bf16[256,6144]{1,0:T(8,128)(2,1)}) custom-call(s32[8,16]{1,0:T(8,128)} %bitcast.18, bf16[512,6144]{1,0:T(8,128)(2,1)} %q_ref.7, bf16[512,6144]{1,0:T(8,128)(2,1)} %k_ref.6, bf16[512,4096]{1,0:T(8,128)(2,1)} %v_ref.9), custom_call_target="tpu_custom_call" | custom-call | flops 1 | bytes 1 | tf_op jit(solution)/shard_map/pack/pallas_call | solution.py:111
  14.1 1.3 collective-permute-start.1
  15.4 9.0 %collective-permute-start.8 = (bf16[64,10240]{1,0:T(8,128)(2,1)}, bf16[64,10240]{1,0:T(8,128)(2,1)}, u32[]{:S(2)}, u32[]{:S(2)}) collective-permute-start(bf16[64,10240]{1,0:T(8,128)(2,1)} %get-tuple-element.67), channel_id=1, source_target_pairs={{0,12},{1,13},{2,14},{3,15},{16,28},{17,29},{18,30},{19,31}} | collective-permute-start | bytes 3932168 | tf_op jit(solution)/shard_map/ppermute | solution.py:35
  24.4 0.0 copy-done.4
  24.4 0.7 copy.17
  25.1 0.7 copy.18
  25.7 8.8 %pool.1 = (bf16[16,10240]{1,0:T(8,128)(2,1)}, f32[512,128]{1,0:T(8,128)}) custom-call(bf16[512,6144]{1,0:T(8,128)(2,1)} %k_ref.6, bf16[512,4096]{1,0:T(8,128)(2,1)} %v_ref.9, f32[32,32]{1,0:T(8,128)} %bitcast.15, f32[32,32]{1,0:T(8,128)} %bitcast.16, f32[3,32,512]{2,1,0:T(8,128)} %bitcast.14), custom_call_target="tpu_custom_call" | custom-call | flops 1 | bytes 1 | tf_op jit(solution)/shard_map/pool/pallas_call | solution.py:163
  34.5 0.0 copy-start.1
  34.5 21.2 %local.1 = (bf16[512,4096]{1,0:T(8,128)(2,1)}, bf16[512,4096]{1,0:T(8,128)(2,1)}, f32[256,128]{1,0:T(8,128)}, f32[512,128]{1,0:T(8,128)}) custom-call(s32[32]{0:T(128)} %win_ref.5, bf16[512,6144]{1,0:T(8,128)(2,1)} %q_ref.7, bf16[512,6144]{1,0:T(8,128)(2,1)} %k_ref.6, bf16[512,4096]{1,0:T(8,128)(2,1)} %v_ref.9, f32[512,128]{1,0:T(8,128)} %get-tuple-element.52.table_ref), custom_call_target="tpu_custom_call" | custom-call | flops 1 | bytes 1 | tf_op jit(solution)/shard_map/local/pallas_call | solution.py:340
  55.7 0.0 collective-permute-done.2.rest_0_.rest_3_
  55.7 1.3 collective-permute-start.3
  57.1 0.1 constant_dynamic-slice_fusion
  57.2 0.1 copy.19
  57.3 14.2 %collective-permute-done.3.rest_7_ = bf16[16,10240]{1,0:T(8,128)(2,1)S(1)} collective-permute-done((bf16[16,10240]{1,0:T(8,128)(2,1)S(1)}, bf16[16,10240]{1,0:T(8,128)(2,1)S(1)}, u32[]{:S(2)}, u32[]{:S(2)}) %collective-permute-start.3) | collective-permute-done | bytes 327712 | tf_op jit(solution)/shard_map/ppermute | solution.py:35
  71.5 0.7 collective-permute-start.4
  72.1 0.2 compare_reduce_fusion
  72.4 0.7 multiply_reduce_fusion
  73.1 0.0 collective-permute-done.4.rest_8_
  73.1 15.0 %collective-permute-start.7 = (bf16[64,10240]{1,0:T(8,128)(2,1)S(1)}, bf16[64,10240]{1,0:T(8,128)(2,1)}, u32[]{:S(2)}, u32[]{:S(2)}) collective-permute-start(bf16[64,10240]{1,0:T(8,128)(2,1)S(1)} %copy-done.7), channel_id=1, source_target_pairs={{0,8},{4,12},{1,9},{5,13},{2,10},{6,14},{3,11},{7,15},{16,24},{20,... | collective-permute-start | bytes 3932168 | tf_op jit(solution)/shard_map/ppermute | solution.py:35
  88.1 0.1 broadcast_and_fusion
  88.2 5.6 %pmax.7 = s32[]{:T(128)} all-reduce(s32[]{:T(128)} %multiply_reduce_fusion), channel_id=1, replica_groups=mesh['parts'=2,'seq'=4,'head'=2,'sub'=2] {'head','sub'}, use_global_device_ids=true, to_apply=%region_1.2 | all-reduce | flops 1 | bytes 8 | tf_op jit(solution)/shard_map/pmax | solution.py:565
  93.8 0.1 broadcast_bitcast_fusion
  93.9 0.3 copy.20
  94.2 0.7 collective-permute-start.5
  94.9 0.1 compare_and_fusion
  95.1 1.0 add_select_fusion.bias_ref
  96.0 0.0 collective-permute-done.5.rest_9_
  96.0 0.0 collective-permute-done.1.q_ref
  96.0 0.7 copy-done.11
  96.8 19.5 %helper.1 = (bf16[1536,128]{1,0:T(8,128)(2,1)}, bf16[4608,128]{1,0:T(8,128)(2,1)}, bf16[2048,128]{1,0:T(8,128)(2,1)S(1)}, f32[32,256]{1,0:T(8,128)}) custom-call(s32[32]{0:T(128)} %win_ref.5, bf16[256,6144]{1,0:T(8,128)(2,1)} %collective-permute-done.1.q_ref, bf16[512,6144]{1,0:T(8,128)(2,1)} %k_ref.6, bf16[512,4096]{1,0:T(8,128)(2,1)} %v_ref.9), custom_call_target="tpu_custom_call" | custom-call | flops 1 | bytes 1 | tf_op jit(solution)/shard_map/helper/pallas_call | solution.py:244
  116.3 4.4 %collective-permute-start.6 = (bf16[1536,128]{1,0:T(8,128)(2,1)}, bf16[1536,128]{1,0:T(8,128)(2,1)S(1)}, u32[]{:S(2)}, u32[]{:S(2)}) collective-permute-start(bf16[1536,128]{1,0:T(8,128)(2,1)} %get-tuple-element.58), channel_id=1, source_target_pairs={{0,4},{4,8},{8,12},{1,5},{5,9},{9,13},{2,6},{6,10},{10,14},{3,7},{... | collective-permute-start | bytes 1179656 | tf_op jit(solution)/shard_map/ppermute | solution.py:35
  120.7 7.2 %collective-permute-start.9 = (f32[32,256]{1,0:T(8,128)}, f32[32,256]{1,0:T(8,128)S(1)}, u32[]{:S(2)}, u32[]{:S(2)}) collective-permute-start(f32[32,256]{1,0:T(8,128)} %get-tuple-element.69), channel_id=1, source_target_pairs={{0,4},{4,8},{8,12},{1,5},{5,9},{9,13},{2,6},{6,10},{10,14},{3,7},{... | collective-permute-start | bytes 98312 | tf_op jit(solution)/shard_map/ppermute | solution.py:35
  128.5 0.0 collective-permute-done.8.rest_2_.rest_5_
  128.5 1.2 collective-permute-done.9.stats_ref
  129.7 0.0 collective-permute-done.7.rest_1_.rest_4_
  129.7 20.5 %collective-permute-start.10 = (bf16[4608,128]{1,0:T(8,128)(2,1)}, bf16[4608,128]{1,0:T(8,128)(2,1)S(1)}, u32[]{:S(2)}, u32[]{:S(2)}) collective-permute-start(bf16[4608,128]{1,0:T(8,128)(2,1)} %get-tuple-element.84), channel_id=1, source_target_pairs={{0,4},{4,8},{8,12},{1,5},{5,9},{9,13},{2,6},{6,10},{10,14},{3,7},{... | collective-permute-start | bytes 3538952 | tf_op jit(solution)/shard_map/ppermute | solution.py:35
  150.2 0.0 collective-permute-done.6.rest_0_
  150.3 0.0 copy-start.2
  150.3 22.5 %far.1 = (bf16[512,4096]{1,0:T(8,128)(2,1)}, f32[256,128]{1,0:T(8,128)}) custom-call(f32[1]{0:T(128)} %bitcast.5.neg_ref, bf16[512,6144]{1,0:T(8,128)(2,1)} %q_ref.7, bf16[512,4096]{1,0:T(8,128)(2,1)} %get-tuple-element.60.win_ref, bf16[512,4096]{1,0:T(8,128)(2,1)} %get-tuple-element.61.own_ref, f32[512,128]{1,0:T(8,128)} %get-tuple-element.52.table_ref, ...), custom_call_target="tpu_custom_call" | custom-call | flops 32768000000 | bytes 25165824 | tf_op jit(solution)/shard_map/far/pallas_call | solution.py:452
  172.8 0.9 conditional.1
  172.8 0.9 broadcast.151
  173.7 1.2 collective-permute-done.10.rest_1_
  174.8 0.9 copy-done
  175.8 5.0 %merge.1 = bf16[512,4096]{1,0:T(8,128)(2,1)} custom-call(s32[32]{0:T(128)S(1)} %copy-done.2, f32[256,128]{1,0:T(8,128)S(1)} %copy-done, bf16[512,4096]{1,0:T(8,128)(2,1)} %get-tuple-element.82.base_ref, bf16[1536,128]{1,0:T(8,128)(2,1)S(1)} %collective-permute-done.6.rest_0_, ...), custom_call_target="tpu_custom_call", output_to_operand_aliasing={{}: (2, {})} | custom-call | flops 1 | bytes 1 | tf_op jit(solution)/shard_map/merge/pallas_call | solution.py:506
  (27 shorter events, 0.1 us)
Async XLA Ops:
  3.1 21.3 %copy-start.4 = (f32[32,32]{1,0:T(8,128)S(1)}, f32[32,32]{1,0:T(8,128)}, u32[]{:S(2)}) copy-start(f32[32,32]{1,0:T(8,128)} %param.14) | copy-start | bytes 12292
  3.1 21.9 %copy-start.5 = (f32[32,32]{1,0:T(8,128)S(1)}, f32[32,32]{1,0:T(8,128)}, u32[]{:S(2)}) copy-start(f32[32,32]{1,0:T(8,128)} %param.15) | copy-start | bytes 12292
  3.1 52.6 %collective-permute-start.2 = (bf16[64,10240]{1,0:T(8,128)(2,1)}, bf16[64,10240]{1,0:T(8,128)(2,1)S(1)}, u32[]{:S(2)}, u32[]{:S(2)}) collective-permute-start(bf16[64,10240]{1,0:T(8,128)(2,1)} %pack.2), channel_id=1, source_target_pairs={{0,4},{4,8},{8,12},{1,5},{5,9},{9,13},{2,6},{6,10},{10,14},{3,7},{... | collective-permute-start | bytes 3932168 | tf_op jit(solution)/shard_map/ppermute | solution.py:35
  14.1 81.9 %collective-permute-start.1 = (bf16[256,6144]{1,0:T(8,128)(2,1)}, bf16[256,6144]{1,0:T(8,128)(2,1)}, u32[]{:S(2)}, u32[]{:S(2)}) collective-permute-start(bf16[256,6144]{1,0:T(8,128)(2,1)} %get-tuple-element.49), channel_id=1, source_target_pairs={{4,0},{8,4},{12,8},{5,1},{9,5},{13,9},{6,2},{10,6},{14,10},{7,3},{... | collective-permute-start | bytes 9437192 | tf_op jit(solution)/shard_map/ppermute | solution.py:35
  15.4 113.1 %collective-permute-start.8 = (bf16[64,10240]{1,0:T(8,128)(2,1)}, bf16[64,10240]{1,0:T(8,128)(2,1)}, u32[]{:S(2)}, u32[]{:S(2)}) collective-permute-start(bf16[64,10240]{1,0:T(8,128)(2,1)} %get-tuple-element.67), channel_id=1, source_target_pairs={{0,12},{1,13},{2,14},{3,15},{16,28},{17,29},{18,30},{19,31}} | collective-permute-start | bytes 3932168 | tf_op jit(solution)/shard_map/ppermute | solution.py:35
  34.5 21.2 %copy-start.8 = (bf16[16,10240]{1,0:T(8,128)(2,1)S(1)}, bf16[16,10240]{1,0:T(8,128)(2,1)}, u32[]{:S(2)}) copy-start(bf16[16,10240]{1,0:T(8,128)(2,1)} %get-tuple-element.76.rest_6_) | copy-start | bytes 983044
  34.5 22.5 %copy-start.3 = (s32[16,8]{0,1:T(8,128)S(1)}, s32[16,8]{0,1:T(8,128)}, u32[]{:S(2)}) copy-start(s32[16,8]{0,1:T(8,128)} %param.17) | copy-start | bytes 1540
  34.5 37.8 %copy-start.1 = (s32[32]{0:T(128)S(1)}, s32[32]{0:T(128)}, u32[]{:S(2)}) copy-start(s32[32]{0:T(128)} %win_ref.5) | copy-start | bytes 388
  34.5 38.5 %copy-start.7 = (bf16[64,10240]{1,0:T(8,128)(2,1)S(1)}, bf16[64,10240]{1,0:T(8,128)(2,1)}, u32[]{:S(2)}) copy-start(bf16[64,10240]{1,0:T(8,128)(2,1)} %get-tuple-element.66) | copy-start | bytes 3932164
  55.7 60.6 %copy-start.6 = (bf16[64,10240]{1,0:T(8,128)(2,1)}, bf16[64,10240]{1,0:T(8,128)(2,1)S(1)}, u32[]{:S(2)}) copy-start(bf16[64,10240]{1,0:T(8,128)(2,1)S(1)} %collective-permute-done.2.rest_0_.rest_3_) | copy-start | bytes 3932164
  55.7 15.7 %collective-permute-start.3 = (bf16[16,10240]{1,0:T(8,128)(2,1)S(1)}, bf16[16,10240]{1,0:T(8,128)(2,1)S(1)}, u32[]{:S(2)}, u32[]{:S(2)}) collective-permute-start(bf16[16,10240]{1,0:T(8,128)(2,1)S(1)} %copy-done.8), channel_id=1, source_target_pairs={{0,4},{4,8},{8,12},{1,5},{5,9},{9,13},{2,6},{6,10},{10,14},{3,7},{... | collective-permute-start | bytes 983048 | tf_op jit(solution)/shard_map/ppermute | solution.py:35
  71.4 22.4 %copy-start.9 = (bf16[16,10240]{1,0:T(8,128)(2,1)}, bf16[16,10240]{1,0:T(8,128)(2,1)S(1)}, u32[]{:S(2)}) copy-start(bf16[16,10240]{1,0:T(8,128)(2,1)S(1)} %collective-permute-done.3.rest_7_) | copy-start | bytes 983044
  71.5 1.6 collective-permute-start.4
  73.1 43.2 %copy-start.10 = (bf16[16,10240]{1,0:T(8,128)(2,1)}, bf16[16,10240]{1,0:T(8,128)(2,1)S(1)}, u32[]{:S(2)}) copy-start(bf16[16,10240]{1,0:T(8,128)(2,1)S(1)} %collective-permute-done.4.rest_8_) | copy-start | bytes 983044
  73.1 56.7 %collective-permute-start.7 = (bf16[64,10240]{1,0:T(8,128)(2,1)S(1)}, bf16[64,10240]{1,0:T(8,128)(2,1)}, u32[]{:S(2)}, u32[]{:S(2)}) collective-permute-start(bf16[64,10240]{1,0:T(8,128)(2,1)S(1)} %copy-done.7), channel_id=1, source_target_pairs={{0,8},{4,12},{1,9},{5,13},{2,10},{6,14},{3,11},{7,15},{16,24},{20,... | collective-permute-start | bytes 3932168 | tf_op jit(solution)/shard_map/ppermute | solution.py:35
  94.2 1.8 collective-permute-start.5
  96.0 0.7 copy-start.11
  116.3 34.0 %collective-permute-start.6 = (bf16[1536,128]{1,0:T(8,128)(2,1)}, bf16[1536,128]{1,0:T(8,128)(2,1)S(1)}, u32[]{:S(2)}, u32[]{:S(2)}) collective-permute-start(bf16[1536,128]{1,0:T(8,128)(2,1)} %get-tuple-element.58), channel_id=1, source_target_pairs={{0,4},{4,8},{8,12},{1,5},{5,9},{9,13},{2,6},{6,10},{10,14},{3,7},{... | collective-permute-start | bytes 1179656 | tf_op jit(solution)/shard_map/ppermute | solution.py:35
  120.7 9.1 %collective-permute-start.9 = (f32[32,256]{1,0:T(8,128)}, f32[32,256]{1,0:T(8,128)S(1)}, u32[]{:S(2)}, u32[]{:S(2)}) collective-permute-start(f32[32,256]{1,0:T(8,128)} %get-tuple-element.69), channel_id=1, source_target_pairs={{0,4},{4,8},{8,12},{1,5},{5,9},{9,13},{2,6},{6,10},{10,14},{3,7},{... | collective-permute-start | bytes 98312 | tf_op jit(solution)/shard_map/ppermute | solution.py:35
  129.7 20.5 %copy-start.12 = (f32[32,256]{1,0:T(8,128)}, f32[32,256]{1,0:T(8,128)S(1)}, u32[]{:S(2)}) copy-start(f32[32,256]{1,0:T(8,128)S(1)} %collective-permute-done.9.stats_ref) | copy-start | bytes 98308
  129.7 45.1 %collective-permute-start.10 = (bf16[4608,128]{1,0:T(8,128)(2,1)}, bf16[4608,128]{1,0:T(8,128)(2,1)S(1)}, u32[]{:S(2)}, u32[]{:S(2)}) collective-permute-start(bf16[4608,128]{1,0:T(8,128)(2,1)} %get-tuple-element.84), channel_id=1, source_target_pairs={{0,4},{4,8},{8,12},{1,5},{5,9},{9,13},{2,6},{6,10},{10,14},{3,7},{... | collective-permute-start | bytes 3538952 | tf_op jit(solution)/shard_map/ppermute | solution.py:35
  150.3 24.6 %copy-start.2 = (s32[32]{0:T(128)S(1)}, s32[32]{0:T(128)}, u32[]{:S(2)}) copy-start(s32[32]{0:T(128)} %win_ref.5) | copy-start | bytes 388
  174.8 0.9 copy-start
